TPU v7x, 32 devices: a whole 2x2x4 slice. The times are simulated.
32 devices in a mesh: wx: 8 (over y, x, core), ny: 4 (over z).
Axes of the slice: x: 2, y: 2, z: 4, core: 2. Of those that a mesh axis runs over, the one named last changes fastest.
Arguments:
- displacement: float32 [3, 32, 6, 512], P(None, 'wx', None, 'ny'), may hold values from -0.1 to 0.1
- velocity: float32 [3, 32, 6, 512], P(None, 'wx', None, 'ny'), may hold values from -1 to 1
- labels: int32 [32, 6, 512], P('wx', None, 'ny'), may hold values from 0 to 7
- bond_mask: int32 [61, 32, 6, 512], P(None, 'wx', None, 'ny'), may hold values 0 or 1
- stiffness: float32 [8], replicated, may hold values from 1 to 10
- critical: float32 [8], replicated, may hold values from 0.02 to 0.2
Outputs:
- final_displacement: float32 [3, 32, 6, 512], P(None, 'wx', None, 'ny')
- final_velocity: float32 [3, 32, 6, 512], P(None, 'wx', None, 'ny')
All inputs are finite; a program needn't handle non-finite values. No bound on the sum of `bond_mask` on one device may be relied on, other than what follows from the above.
Results may differ from a plain program's by a relative error of at most 0.00002.
Values sent between devices are 32-bit elements; how exact they have to be, the bound alone decides.
A program may use at most 64 MiB of HBM per device.

v0:
```python
import math

import jax
import jax.numpy as jnp
from jax import lax
from jax.sharding import PartitionSpec as P

STEPS = 3
MATS = 8


time_step = 0.05


def with_halo(block, sides, width):
    for axis, dim in sides:
        count = lax.axis_size(axis)
        forward = [(i, i + 1) for i in range(count - 1)]
        backward = [(target, source) for source, target in forward]
        low = lax.ppermute(
            lax.slice_in_dim(block, block.shape[dim] - width, None, axis=dim), axis, forward
        )
        high = lax.ppermute(lax.slice_in_dim(block, 0, width, axis=dim), axis, backward)
        block = jnp.concatenate([low, block, high], axis=dim)
    return block


def shifted(value, axis, steps):
    count = lax.axis_size(axis)
    initial, last = (max(0, -steps), min(count, count - steps))
    return lax.ppermute(value, axis, [(source, source + steps) for source in range(initial, last)])


def bond_offsets():
    chosen = []
    for step_x in range(0, 4):
        for step_z in range(-3, 4):
            for step_y in range(-3, 4):
                if step_x * step_x + step_z * step_z + step_y * step_y <= 9:
                    if step_x > 0 or (step_x == 0 and (step_z > 0 or (step_z == 0 and step_y > 0))):
                        chosen.append((step_x, step_z, step_y))
    return chosen


def node_material(labels, stiffness, critical):
    modulus = jnp.zeros(labels.shape, jnp.float32)
    strain_limit = jnp.zeros(labels.shape, jnp.float32)
    for material in range(MATS):
        matches = labels == material
        modulus = jnp.where(matches, stiffness[material], modulus)
        strain_limit = jnp.where(matches, critical[material], strain_limit)
    return (modulus, strain_limit)


def pair_force(
    offset, source, target, modulus_here, modulus_there, limit_here, limit_there, intact
):
    length = math.sqrt(offset[0] * offset[0] + offset[1] * offset[1] + offset[2] * offset[2])
    relative = [
        float(offset[component]) + target[component] - source[component] for component in range(3)
    ]
    distance = jnp.sqrt(
        relative[0] * relative[0] + relative[1] * relative[1] + relative[2] * relative[2]
    )
    stretch = (distance - length) / length
    pair_modulus = 2.0 * modulus_here * modulus_there / (modulus_here + modulus_there)
    pair_limit = 0.5 * (limit_here + limit_there)
    ratio = stretch / pair_limit
    magnitude = intact * pair_modulus * stretch / (1.0 + ratio * ratio) / (length * length)
    return jnp.stack([magnitude * part for part in relative])


def extend(source):
    widened = with_halo(source, (("ny", 3),), 3)
    front_rows = shifted(widened[:, :3], "wx", -1)
    return jnp.concatenate([widened, front_rows], axis=1)


def send_back(spread, rows_x, rows_y):
    returned = shifted(spread[:, rows_x:], "wx", 1)
    central = spread[:, :rows_x].at[:, :3].add(returned)
    lower_rim = shifted(central[:, :, :, :3], "ny", -1)
    upper_rim = shifted(central[:, :, :, rows_y + 3 :], "ny", 1)
    interior = central[:, :, :, 3 : 3 + rows_y]
    interior = interior.at[:, :, :, rows_y - 3 :].add(lower_rim)
    return interior.at[:, :, :, :3].add(upper_rim)


def on_device(displacement, velocity, labels, bond_mask, stiffness, critical):
    rows_x, rows_z, rows_y = labels.shape
    modulus, strain_limit = node_material(labels, stiffness, critical)
    material_ext = extend(jnp.stack([modulus, strain_limit]))
    material_ext = jnp.pad(material_ext, ((0, 0), (0, 0), (3, 3), (0, 0)))
    extent_x = rows_x * lax.axis_size("wx")
    extent_y = rows_y * lax.axis_size("ny")
    global_x = lax.axis_index("wx") * rows_x + jnp.arange(rows_x, dtype=jnp.int32).reshape(
        rows_x, 1, 1
    )
    global_y = lax.axis_index("ny") * rows_y + jnp.arange(rows_y, dtype=jnp.int32).reshape(
        1, 1, rows_y
    )
    depth_index = jnp.arange(rows_z, dtype=jnp.int32).reshape(1, rows_z, 1)
    offsets = bond_offsets()
    intact_list = []
    for number, offset in enumerate(offsets):
        step_x, step_z, step_y = offset
        inside = global_x + step_x < extent_x
        inside = inside & (depth_index + step_z >= 0) & (depth_index + step_z < rows_z)
        inside = inside & (global_y + step_y >= 0) & (global_y + step_y < extent_y)
        intact_list.append(jnp.where(inside, bond_mask[number], 0).astype(jnp.float32))
    for repeat in range(STEPS):
        disp_ext = jnp.pad(extend(displacement), ((0, 0), (0, 0), (3, 3), (0, 0)))
        force_here = jnp.zeros(displacement.shape, jnp.float32)
        spread = jnp.zeros(disp_ext.shape, jnp.float32)
        for number, offset in enumerate(offsets):
            step_x, step_z, step_y = offset
            low_z, low_y = (3 + step_z, 3 + step_y)
            target = disp_ext[
                :, step_x : step_x + rows_x, low_z : low_z + rows_z, low_y : low_y + rows_y
            ]
            there = material_ext[
                :, step_x : step_x + rows_x, low_z : low_z + rows_z, low_y : low_y + rows_y
            ]
            force = pair_force(
                offset,
                displacement,
                target,
                modulus,
                there[0],
                strain_limit,
                there[1],
                intact_list[number],
            )
            force_here = force_here + force
            spread = spread + jnp.pad(
                -force, ((0, 0), (step_x, 3 - step_x), (low_z, 3 - step_z), (low_y, 3 - step_y))
            )
        spread = spread[:, :, 3 : 3 + rows_z, :]
        force = force_here + send_back(spread, rows_x, rows_y)
        velocity = velocity + time_step * force
        displacement = displacement + time_step * velocity
    return (displacement, velocity)


def solution(mesh):
    in_specs = (
        P(None, "wx", None, "ny"),
        P(None, "wx", None, "ny"),
        P("wx", None, "ny"),
        P(None, "wx", None, "ny"),
        P(),
        P(),
    )
    out_specs = (P(None, "wx", None, "ny"), P(None, "wx", None, "ny"))
    return jax.shard_map(
        on_device, mesh=mesh, in_specs=in_specs, out_specs=out_specs, check_vma=False
    )
```

profile of v0, /device:TPU:4, one launch (start us, length us, event | category | flops | bytes accessed | tf_op | source)
XLA Modules:
  0.0 150.1 jit_solution(11847981649774724518)
XLA Ops:
  3.7 5.0 %select_select_fusion = (f32[4,6,128]{2,0,1:T(4,128)S(1)}, pred[4,6,128]{2,0,1:T(4,128)(4,1)S(1)}, pred[4,6,128]{2,0,1:T(4,128)(4,1)S(1)}, pred[4,6,128]{2,0,1:T...) fusion(f32[]{:T(128)} %bitcast.17, f32[]{:T(128)} %bitcast.16, ...), kind=kLoop, calls=%fused_computation.4769 | loop fusion | flops 49152 | bytes 49184 | tf_op jit(solution)/shard_map/jit(_where)/select_n | solution.py:51
  8.7 4.9 %select_select_fusion.1 = f32[4,6,128]{2,0,1:T(4,128)S(1)} fusion(pred[4,6,128]{2,0,1:T(4,128)(4,1)S(1)} %get-tuple-element.563, pred[4,6,128]{2,0,1:T(4,128)(4,1)S(1)} %get-tuple-element.562, pred[4,6,128]{2,0,1:T(4,128)(4,1)S(1)} %get-tuple-element.561, pred[4,6,128]{2,0,1:T(4,128)(4,1)S(1)} %get-tuple-element.560, ...), kind=kLoop, calls=%fused_computation.4770 | loop fusion | flops 24576 | bytes 36896 | tf_op jit(solution)/shard_map/jit(_where)/select_n | solution.py:50
  13.7 3.6 %collective-permute-start.2 = (f32[2,4,6,3]{3,1,2,0:T(4,128)S(1)}, f32[2,4,6,3]{3,1,2,0:T(4,128)S(1)}, u32[]{:S(2)}, u32[]{:S(2)}) collective-permute-start(f32[2,4,6,3]{3,1,2,0:T(4,128)S(1)} %get-tuple-element.1366), channel_id=1, source_target_pairs={{0,1},{1,2},{2,3},{4,5},{5,6},{6,7},{8,9},{9,10},{10,11},{12,13},{... | collective-permute-start | bytes 1736 | tf_op jit(solution)/shard_map/ppermute | solution.py:20
  18.7 4.5 %collective-permute-start.4 = (f32[3,4,6,3]{3,1,2,0:T(4,128)S(1)}, f32[3,4,6,3]{3,1,2,0:T(4,128)S(1)}, u32[]{:S(2)}, u32[]{:S(2)}) collective-permute-start(f32[3,4,6,3]{3,1,2,0:T(4,128)S(1)} %get-tuple-element.1364), channel_id=1, source_target_pairs={{0,1},{1,2},{2,3},{4,5},{5,6},{6,7},{8,9},{9,10},{10,11},{12,13},{... | collective-permute-start | bytes 2600 | tf_op jit(solution)/shard_map/ppermute | solution.py:20
  25.1 1.9 %collective-permute-start.3 = (f32[2,3,6,134]{3,1,2,0:T(4,128)S(1)}, f32[2,3,6,134]{3,1,2,0:T(4,128)S(1)}, u32[]{:S(2)}, u32[]{:S(2)}) collective-permute-start(f32[2,3,6,134]{3,1,2,0:T(4,128)S(1)} %pad_maximum_fusion.10), channel_id=1, source_target_pairs={{4,0},{8,4},{12,8},{16,12},{20,16},{24,20},{28,24},{5,1},{9,5},{13... | collective-permute-start | bytes 57896 | tf_op jit(solution)/shard_map/ppermute | solution.py:31
  27.0 2.1 %collective-permute-done.1 = f32[3,4,6,3]{3,1,2,0:T(4,128)S(1)} collective-permute-done((f32[3,4,6,3]{3,1,2,0:T(4,128)S(1)}, f32[3,4,6,3]{3,1,2,0:T(4,128)S(1)}, u32[]{:S(2)}, u32[]{:S(2)}) %collective-permute-start.1) | collective-permute-done | bytes 896 | tf_op jit(solution)/shard_map/ppermute | solution.py:23
  45.1 2.5 %pad_add_fusion.2 = f32[3,7,12,134]{3,1,2,0:T(8,128)S(1)} fusion(f32[3,4,6,128]{3,1,2,0:T(4,128)S(1)} %fusion.122, f32[3,4,6,128]{3,1,2,0:T(4,128)S(1)} %fusion.123, f32[3,4,6,128]{3,1,2,0:T(4,128)S(1)} %fusion.124, f32[3,4,6,128]{3,1,2,0:T(4,128)S(1)} %fusion.125, f32[3,4,6,128]{3,1,2,0:T(4,128)S(1)} %fusion.126, f32[3,4,6,128]{3,1,2,0:T(4,128)S(1)} %fusion.127, ...), kind=kLoop, calls=%fused_computation.519 | loop fusion | flops 2026080 | bytes 2383776 | tf_op jit(solution)/shard_map/add | solution.py:135
  47.6 2.4 %collective-permute-start.6 = (f32[3,3,6,134]{3,1,2,0:T(4,128)S(1)}, f32[3,3,6,134]{3,1,2,0:T(4,128)S(1)}, u32[]{:S(2)}, u32[]{:S(2)}) collective-permute-start(f32[3,3,6,134]{3,1,2,0:T(4,128)S(1)} %slice.5429), channel_id=1, source_target_pairs={{0,4},{4,8},{8,12},{12,16},{16,20},{20,24},{24,28},{1,5},{5,9},{9,... | collective-permute-start | bytes 86840 | tf_op jit(solution)/shard_map/ppermute | solution.py:31
  50.1 4.1 %collective-permute-done.6 = f32[3,3,6,134]{3,1,2,0:T(4,128)S(1)} collective-permute-done((f32[3,3,6,134]{3,1,2,0:T(4,128)S(1)}, f32[3,3,6,134]{3,1,2,0:T(4,128)S(1)}, u32[]{:S(2)}, u32[]{:S(2)}) %collective-permute-start.6) | collective-permute-done | bytes 28976 | tf_op jit(solution)/shard_map/ppermute | solution.py:31
  56.0 4.8 %collective-permute-start.8 = (f32[3,4,6,3]{3,1,2,0:T(4,128)S(1)}, f32[3,4,6,3]{3,1,2,0:T(4,128)S(1)}, u32[]{:S(2)}, u32[]{:S(2)}) collective-permute-start(f32[3,4,6,3]{3,1,2,0:T(4,128)S(1)} %get-tuple-element.1350), channel_id=1, source_target_pairs={{0,1},{1,2},{2,3},{4,5},{5,6},{6,7},{8,9},{9,10},{10,11},{12,13},{... | collective-permute-start | bytes 2600 | tf_op jit(solution)/shard_map/ppermute | solution.py:31
  60.8 2.8 %scatter-add.31 = f32[3,4,6,128]{3,1,2,0:T(4,128)S(1)} dynamic-update-slice(f32[3,4,6,128]{3,1,2,0:T(4,128)S(1)} %slice.5430, f32[3,4,6,3]{3,1,2,0:T(4,128)S(1)} %slice_add_fusion.8, s32[]{:T(128)} %constant.792.clone.1, s32[]{:T(128)} %constant.792.clone.1, s32[]{:T(128)} %constant.792.clone.1, s32[]{:T(128)} %constant.824.clone.1) | dynamic-update-slice | bytes 1732 | tf_op jit(solution)/shard_map/scatter-add | solution.py:85
  65.3 3.9 %collective-permute-start.10 = (f32[3,4,6,3]{3,1,2,0:T(4,128)S(1)}, f32[3,4,6,3]{3,1,2,0:T(4,128)S(1)}, u32[]{:S(2)}, u32[]{:S(2)}) collective-permute-start(f32[3,4,6,3]{3,1,2,0:T(4,128)S(1)} %get-tuple-element.1362), channel_id=1, source_target_pairs={{0,1},{1,2},{2,3},{4,5},{5,6},{6,7},{8,9},{9,10},{10,11},{12,13},{... | collective-permute-start | bytes 2600 | tf_op jit(solution)/shard_map/ppermute | solution.py:20
  70.8 4.2 %collective-permute-done.9 = f32[3,4,6,3]{3,1,2,0:T(4,128)S(1)} collective-permute-done((f32[3,4,6,3]{3,1,2,0:T(4,128)S(1)}, f32[3,4,6,3]{3,1,2,0:T(4,128)S(1)}, u32[]{:S(2)}, u32[]{:S(2)}) %collective-permute-start.9) | collective-permute-done | bytes 896 | tf_op jit(solution)/shard_map/ppermute | solution.py:23
  89.1 2.5 %pad_add_fusion.1 = f32[3,7,12,134]{3,1,2,0:T(8,128)S(1)} fusion(f32[3,4,6,128]{3,1,2,0:T(4,128)S(1)} %fusion.61, f32[3,4,6,128]{3,1,2,0:T(4,128)S(1)} %fusion.62, f32[3,4,6,128]{3,1,2,0:T(4,128)S(1)} %fusion.63, f32[3,4,6,128]{3,1,2,0:T(4,128)S(1)} %fusion.64, f32[3,4,6,128]{3,1,2,0:T(4,128)S(1)} %fusion.65, f32[3,4,6,128]{3,1,2,0:T(4,128)S(1)} %fusion.66, ...), kind=kLoop, calls=%fused_computation.518 | loop fusion | flops 2026080 | bytes 2383776 | tf_op jit(solution)/shard_map/add | solution.py:135
  91.6 2.2 %collective-permute-start.12 = (f32[3,3,6,134]{3,1,2,0:T(4,128)S(1)}, f32[3,3,6,134]{3,1,2,0:T(4,128)S(1)}, u32[]{:S(2)}, u32[]{:S(2)}) collective-permute-start(f32[3,3,6,134]{3,1,2,0:T(4,128)S(1)} %slice.5491), channel_id=1, source_target_pairs={{0,4},{4,8},{8,12},{12,16},{16,20},{20,24},{24,28},{1,5},{5,9},{9,... | collective-permute-start | bytes 86840 | tf_op jit(solution)/shard_map/ppermute | solution.py:31
  93.8 4.4 %collective-permute-done.12 = f32[3,3,6,134]{3,1,2,0:T(4,128)S(1)} collective-permute-done((f32[3,3,6,134]{3,1,2,0:T(4,128)S(1)}, f32[3,3,6,134]{3,1,2,0:T(4,128)S(1)}, u32[]{:S(2)}, u32[]{:S(2)}) %collective-permute-start.12) | collective-permute-done | bytes 28976 | tf_op jit(solution)/shard_map/ppermute | solution.py:31
  100.0 4.8 %collective-permute-start.14 = (f32[3,4,6,3]{3,1,2,0:T(4,128)S(1)}, f32[3,4,6,3]{3,1,2,0:T(4,128)S(1)}, u32[]{:S(2)}, u32[]{:S(2)}) collective-permute-start(f32[3,4,6,3]{3,1,2,0:T(4,128)S(1)} %get-tuple-element.1345), channel_id=1, source_target_pairs={{0,1},{1,2},{2,3},{4,5},{5,6},{6,7},{8,9},{9,10},{10,11},{12,13},{... | collective-permute-start | bytes 2600 | tf_op jit(solution)/shard_map/ppermute | solution.py:31
  104.8 2.8 %scatter-add.36 = f32[3,4,6,128]{3,1,2,0:T(4,128)S(1)} dynamic-update-slice(f32[3,4,6,128]{3,1,2,0:T(4,128)S(1)} %slice.5492, f32[3,4,6,3]{3,1,2,0:T(4,128)S(1)} %slice_add_fusion.6, s32[]{:T(128)} %constant.792.clone.1, s32[]{:T(128)} %constant.792.clone.1, s32[]{:T(128)} %constant.792.clone.1, s32[]{:T(128)} %constant.824.clone.1) | dynamic-update-slice | bytes 1732 | tf_op jit(solution)/shard_map/scatter-add | solution.py:85
  108.9 3.5 %collective-permute-start.16 = (f32[3,4,6,3]{3,1,2,0:T(4,128)S(1)}, f32[3,4,6,3]{3,1,2,0:T(4,128)S(1)}, u32[]{:S(2)}, u32[]{:S(2)}) collective-permute-start(f32[3,4,6,3]{3,1,2,0:T(4,128)S(1)} %get-tuple-element.1360), channel_id=1, source_target_pairs={{0,1},{1,2},{2,3},{4,5},{5,6},{6,7},{8,9},{9,10},{10,11},{12,13},{... | collective-permute-start | bytes 2600 | tf_op jit(solution)/shard_map/ppermute | solution.py:20
  114.0 4.2 %collective-permute-done.15 = f32[3,4,6,3]{3,1,2,0:T(4,128)S(1)} collective-permute-done((f32[3,4,6,3]{3,1,2,0:T(4,128)S(1)}, f32[3,4,6,3]{3,1,2,0:T(4,128)S(1)}, u32[]{:S(2)}, u32[]{:S(2)}) %collective-permute-start.15) | collective-permute-done | bytes 896 | tf_op jit(solution)/shard_map/ppermute | solution.py:23
  129.9 2.5 %pad_add_fusion = f32[3,7,12,134]{3,1,2,0:T(8,128)S(1)} fusion(f32[3,4,6,128]{3,1,2,0:T(4,128)S(1)} %fusion, f32[3,4,6,128]{3,1,2,0:T(4,128)S(1)} %fusion.1, f32[3,4,6,128]{3,1,2,0:T(4,128)S(1)} %fusion.2, f32[3,4,6,128]{3,1,2,0:T(4,128)S(1)} %fusion.3, f32[3,4,6,128]{3,1,2,0:T(4,128)S(1)} %fusion.4, f32[3,4,6,128]{3,1,2,0:T(4,128)S(1)} %fusion.5, ...), kind=kLoop, calls=%fused_computation.517 | loop fusion | flops 2026080 | bytes 2383776 | tf_op jit(solution)/shard_map/add | solution.py:135
  134.3 4.7 %collective-permute-done.18 = f32[3,3,6,134]{3,1,2,0:T(4,128)S(1)} collective-permute-done((f32[3,3,6,134]{3,1,2,0:T(4,128)S(1)}, f32[3,3,6,134]{3,1,2,0:T(4,128)S(1)}, u32[]{:S(2)}, u32[]{:S(2)}) %collective-permute-start.18) | collective-permute-done | bytes 28976 | tf_op jit(solution)/shard_map/ppermute | solution.py:31
  140.8 4.5 %collective-permute-start.20 = (f32[3,4,6,3]{3,1,2,0:T(4,128)S(1)}, f32[3,4,6,3]{3,1,2,0:T(4,128)S(1)}, u32[]{:S(2)}, u32[]{:S(2)}) collective-permute-start(f32[3,4,6,3]{3,1,2,0:T(4,128)S(1)} %get-tuple-element.1340), channel_id=1, source_target_pairs={{0,1},{1,2},{2,3},{4,5},{5,6},{6,7},{8,9},{9,10},{10,11},{12,13},{... | collective-permute-start | bytes 2600 | tf_op jit(solution)/shard_map/ppermute | solution.py:31
  145.3 2.8 %scatter-add.41 = f32[3,4,6,128]{3,1,2,0:T(4,128)S(1)} dynamic-update-slice(f32[3,4,6,128]{3,1,2,0:T(4,128)S(1)} %slice.5554, f32[3,4,6,3]{3,1,2,0:T(4,128)S(1)} %slice_add_fusion.4, s32[]{:T(128)} %constant.792.clone.1, s32[]{:T(128)} %constant.792.clone.1, s32[]{:T(128)} %constant.792.clone.1, s32[]{:T(128)} %constant.824.clone.1) | dynamic-update-slice | bytes 1732 | tf_op jit(solution)/shard_map/scatter-add | solution.py:85
  (510 shorter events, 60.3 us)
Async XLA Ops:
  13.6 17.6 %copy-start.1 = (s32[61,4,6,128]{3,1,2,0:T(4,128)S(1)}, s32[61,4,6,128]{3,1,2,0:T(4,128)}, u32[]{:S(2)}) copy-start(s32[61,4,6,128]{3,1,2,0:T(4,128)} %param.27) | copy-start | bytes 2248708
  13.7 11.2 %collective-permute-start.2 = (f32[2,4,6,3]{3,1,2,0:T(4,128)S(1)}, f32[2,4,6,3]{3,1,2,0:T(4,128)S(1)}, u32[]{:S(2)}, u32[]{:S(2)}) collective-permute-start(f32[2,4,6,3]{3,1,2,0:T(4,128)S(1)} %get-tuple-element.1366), channel_id=1, source_target_pairs={{0,1},{1,2},{2,3},{4,5},{5,6},{6,7},{8,9},{9,10},{10,11},{12,13},{... | collective-permute-start | bytes 1736 | tf_op jit(solution)/shard_map/ppermute | solution.py:20
  17.3 7.6 %collective-permute-start = (f32[2,4,6,3]{3,1,2,0:T(4,128)S(1)}, f32[2,4,6,3]{3,1,2,0:T(4,128)S(1)}, u32[]{:S(2)}, u32[]{:S(2)}) collective-permute-start(f32[2,4,6,3]{3,1,2,0:T(4,128)S(1)} %get-tuple-element.1367), channel_id=1, source_target_pairs={{1,0},{2,1},{3,2},{5,4},{6,5},{7,6},{9,8},{10,9},{11,10},{13,12},{... | collective-permute-start | bytes 1736 | tf_op jit(solution)/shard_map/ppermute | solution.py:23
  18.7 8.3 %collective-permute-start.4 = (f32[3,4,6,3]{3,1,2,0:T(4,128)S(1)}, f32[3,4,6,3]{3,1,2,0:T(4,128)S(1)}, u32[]{:S(2)}, u32[]{:S(2)}) collective-permute-start(f32[3,4,6,3]{3,1,2,0:T(4,128)S(1)} %get-tuple-element.1364), channel_id=1, source_target_pairs={{0,1},{1,2},{2,3},{4,5},{5,6},{6,7},{8,9},{9,10},{10,11},{12,13},{... | collective-permute-start | bytes 2600 | tf_op jit(solution)/shard_map/ppermute | solution.py:20
  23.3 5.9 %collective-permute-start.1 = (f32[3,4,6,3]{3,1,2,0:T(4,128)S(1)}, f32[3,4,6,3]{3,1,2,0:T(4,128)S(1)}, u32[]{:S(2)}, u32[]{:S(2)}) collective-permute-start(f32[3,4,6,3]{3,1,2,0:T(4,128)S(1)} %get-tuple-element.1365), channel_id=1, source_target_pairs={{1,0},{2,1},{3,2},{5,4},{6,5},{7,6},{9,8},{10,9},{11,10},{13,12},{... | collective-permute-start | bytes 2600 | tf_op jit(solution)/shard_map/ppermute | solution.py:23
  25.1 9.1 %collective-permute-start.3 = (f32[2,3,6,134]{3,1,2,0:T(4,128)S(1)}, f32[2,3,6,134]{3,1,2,0:T(4,128)S(1)}, u32[]{:S(2)}, u32[]{:S(2)}) collective-permute-start(f32[2,3,6,134]{3,1,2,0:T(4,128)S(1)} %pad_maximum_fusion.10), channel_id=1, source_target_pairs={{4,0},{8,4},{12,8},{16,12},{20,16},{24,20},{28,24},{5,1},{9,5},{13... | collective-permute-start | bytes 57896 | tf_op jit(solution)/shard_map/ppermute | solution.py:31
  29.3 5.0 %collective-permute-start.5 = (f32[3,3,6,134]{3,1,2,0:T(4,128)S(1)}, f32[3,3,6,134]{3,1,2,0:T(4,128)S(1)}, u32[]{:S(2)}, u32[]{:S(2)}) collective-permute-start(f32[3,3,6,134]{3,1,2,0:T(4,128)S(1)} %pad_maximum_fusion.8), channel_id=1, source_target_pairs={{4,0},{8,4},{12,8},{16,12},{20,16},{24,20},{28,24},{5,1},{9,5},{13... | collective-permute-start | bytes 86840 | tf_op jit(solution)/shard_map/ppermute | solution.py:31
  36.0 8.8 %copy-start.21 = (f32[1,4,6,128]{3,1,2,0:T(4,128)}, f32[1,4,6,128]{3,1,2,0:T(4,128)S(1)}, u32[]{:S(2)}) copy-start(f32[1,4,6,128]{3,1,2,0:T(4,128)S(1)} %get-tuple-element.552) | copy-start | bytes 36868
  47.6 6.6 %collective-permute-start.6 = (f32[3,3,6,134]{3,1,2,0:T(4,128)S(1)}, f32[3,3,6,134]{3,1,2,0:T(4,128)S(1)}, u32[]{:S(2)}, u32[]{:S(2)}) collective-permute-start(f32[3,3,6,134]{3,1,2,0:T(4,128)S(1)} %slice.5429), channel_id=1, source_target_pairs={{0,4},{4,8},{8,12},{12,16},{16,20},{20,24},{24,28},{1,5},{5,9},{9,... | collective-permute-start | bytes 86840 | tf_op jit(solution)/shard_map/ppermute | solution.py:31
  54.6 6.2 %collective-permute-start.7 = (f32[3,4,6,3]{3,1,2,0:T(4,128)S(1)}, f32[3,4,6,3]{3,1,2,0:T(4,128)S(1)}, u32[]{:S(2)}, u32[]{:S(2)}) collective-permute-start(f32[3,4,6,3]{3,1,2,0:T(4,128)S(1)} %get-tuple-element.1351), channel_id=1, source_target_pairs={{1,0},{2,1},{3,2},{5,4},{6,5},{7,6},{9,8},{10,9},{11,10},{13,12},{... | collective-permute-start | bytes 2600 | tf_op jit(solution)/shard_map/ppermute | solution.py:31
  55.9 8.2 %copy-start.16 = (f32[1,4,6,128]{3,1,2,0:T(4,128)S(1)}, f32[1,4,6,128]{3,1,2,0:T(4,128)}, u32[]{:S(2)}) copy-start(f32[1,4,6,128]{3,1,2,0:T(4,128)} %copy-done.15) | copy-start | bytes 36868
  56.0 7.6 %collective-permute-start.8 = (f32[3,4,6,3]{3,1,2,0:T(4,128)S(1)}, f32[3,4,6,3]{3,1,2,0:T(4,128)S(1)}, u32[]{:S(2)}, u32[]{:S(2)}) collective-permute-start(f32[3,4,6,3]{3,1,2,0:T(4,128)S(1)} %get-tuple-element.1350), channel_id=1, source_target_pairs={{0,1},{1,2},{2,3},{4,5},{5,6},{6,7},{8,9},{9,10},{10,11},{12,13},{... | collective-permute-start | bytes 2600 | tf_op jit(solution)/shard_map/ppermute | solution.py:31
  65.3 5.5 %collective-permute-start.10 = (f32[3,4,6,3]{3,1,2,0:T(4,128)S(1)}, f32[3,4,6,3]{3,1,2,0:T(4,128)S(1)}, u32[]{:S(2)}, u32[]{:S(2)}) collective-permute-start(f32[3,4,6,3]{3,1,2,0:T(4,128)S(1)} %get-tuple-element.1362), channel_id=1, source_target_pairs={{0,1},{1,2},{2,3},{4,5},{5,6},{6,7},{8,9},{9,10},{10,11},{12,13},{... | collective-permute-start | bytes 2600 | tf_op jit(solution)/shard_map/ppermute | solution.py:20
  69.2 5.9 %collective-permute-start.9 = (f32[3,4,6,3]{3,1,2,0:T(4,128)S(1)}, f32[3,4,6,3]{3,1,2,0:T(4,128)S(1)}, u32[]{:S(2)}, u32[]{:S(2)}) collective-permute-start(f32[3,4,6,3]{3,1,2,0:T(4,128)S(1)} %get-tuple-element.1363), channel_id=1, source_target_pairs={{1,0},{2,1},{3,2},{5,4},{6,5},{7,6},{9,8},{10,9},{11,10},{13,12},{... | collective-permute-start | bytes 2600 | tf_op jit(solution)/shard_map/ppermute | solution.py:23
  75.2 3.9 %collective-permute-start.11 = (f32[3,3,6,134]{3,1,2,0:T(4,128)S(1)}, f32[3,3,6,134]{3,1,2,0:T(4,128)S(1)}, u32[]{:S(2)}, u32[]{:S(2)}) collective-permute-start(f32[3,3,6,134]{3,1,2,0:T(4,128)S(1)} %pad_maximum_fusion.6), channel_id=1, source_target_pairs={{4,0},{8,4},{12,8},{16,12},{20,16},{24,20},{28,24},{5,1},{9,5},{13... | collective-permute-start | bytes 86840 | tf_op jit(solution)/shard_map/ppermute | solution.py:31
  91.6 6.6 %collective-permute-start.12 = (f32[3,3,6,134]{3,1,2,0:T(4,128)S(1)}, f32[3,3,6,134]{3,1,2,0:T(4,128)S(1)}, u32[]{:S(2)}, u32[]{:S(2)}) collective-permute-start(f32[3,3,6,134]{3,1,2,0:T(4,128)S(1)} %slice.5491), channel_id=1, source_target_pairs={{0,4},{4,8},{8,12},{12,16},{16,20},{20,24},{24,28},{1,5},{5,9},{9,... | collective-permute-start | bytes 86840 | tf_op jit(solution)/shard_map/ppermute | solution.py:31
  98.6 6.2 %collective-permute-start.13 = (f32[3,4,6,3]{3,1,2,0:T(4,128)S(1)}, f32[3,4,6,3]{3,1,2,0:T(4,128)S(1)}, u32[]{:S(2)}, u32[]{:S(2)}) collective-permute-start(f32[3,4,6,3]{3,1,2,0:T(4,128)S(1)} %get-tuple-element.1346), channel_id=1, source_target_pairs={{1,0},{2,1},{3,2},{5,4},{6,5},{7,6},{9,8},{10,9},{11,10},{13,12},{... | collective-permute-start | bytes 2600 | tf_op jit(solution)/shard_map/ppermute | solution.py:31
  100.0 7.6 %collective-permute-start.14 = (f32[3,4,6,3]{3,1,2,0:T(4,128)S(1)}, f32[3,4,6,3]{3,1,2,0:T(4,128)S(1)}, u32[]{:S(2)}, u32[]{:S(2)}) collective-permute-start(f32[3,4,6,3]{3,1,2,0:T(4,128)S(1)} %get-tuple-element.1345), channel_id=1, source_target_pairs={{0,1},{1,2},{2,3},{4,5},{5,6},{6,7},{8,9},{9,10},{10,11},{12,13},{... | collective-permute-start | bytes 2600 | tf_op jit(solution)/shard_map/ppermute | solution.py:31
  108.9 5.1 %collective-permute-start.16 = (f32[3,4,6,3]{3,1,2,0:T(4,128)S(1)}, f32[3,4,6,3]{3,1,2,0:T(4,128)S(1)}, u32[]{:S(2)}, u32[]{:S(2)}) collective-permute-start(f32[3,4,6,3]{3,1,2,0:T(4,128)S(1)} %get-tuple-element.1360), channel_id=1, source_target_pairs={{0,1},{1,2},{2,3},{4,5},{5,6},{6,7},{8,9},{9,10},{10,11},{12,13},{... | collective-permute-start | bytes 2600 | tf_op jit(solution)/shard_map/ppermute | solution.py:20
  112.4 5.9 %collective-permute-start.15 = (f32[3,4,6,3]{3,1,2,0:T(4,128)S(1)}, f32[3,4,6,3]{3,1,2,0:T(4,128)S(1)}, u32[]{:S(2)}, u32[]{:S(2)}) collective-permute-start(f32[3,4,6,3]{3,1,2,0:T(4,128)S(1)} %get-tuple-element.1361), channel_id=1, source_target_pairs={{1,0},{2,1},{3,2},{5,4},{6,5},{7,6},{9,8},{10,9},{11,10},{13,12},{... | collective-permute-start | bytes 2600 | tf_op jit(solution)/shard_map/ppermute | solution.py:23
  118.3 3.9 %collective-permute-start.17 = (f32[3,3,6,134]{3,1,2,0:T(4,128)S(1)}, f32[3,3,6,134]{3,1,2,0:T(4,128)S(1)}, u32[]{:S(2)}, u32[]{:S(2)}) collective-permute-start(f32[3,3,6,134]{3,1,2,0:T(4,128)S(1)} %pad_maximum_fusion.4), channel_id=1, source_target_pairs={{4,0},{8,4},{12,8},{16,12},{20,16},{24,20},{28,24},{5,1},{9,5},{13... | collective-permute-start | bytes 86840 | tf_op jit(solution)/shard_map/ppermute | solution.py:31
  132.4 6.6 %collective-permute-start.18 = (f32[3,3,6,134]{3,1,2,0:T(4,128)S(1)}, f32[3,3,6,134]{3,1,2,0:T(4,128)S(1)}, u32[]{:S(2)}, u32[]{:S(2)}) collective-permute-start(f32[3,3,6,134]{3,1,2,0:T(4,128)S(1)} %slice.5553), channel_id=1, source_target_pairs={{0,4},{4,8},{8,12},{12,16},{16,20},{20,24},{24,28},{1,5},{5,9},{9,... | collective-permute-start | bytes 86840 | tf_op jit(solution)/shard_map/ppermute | solution.py:31
  139.4 5.9 %collective-permute-start.19 = (f32[3,4,6,3]{3,1,2,0:T(4,128)S(1)}, f32[3,4,6,3]{3,1,2,0:T(4,128)S(1)}, u32[]{:S(2)}, u32[]{:S(2)}) collective-permute-start(f32[3,4,6,3]{3,1,2,0:T(4,128)S(1)} %get-tuple-element.1341), channel_id=1, source_target_pairs={{1,0},{2,1},{3,2},{5,4},{6,5},{7,6},{9,8},{10,9},{11,10},{13,12},{... | collective-permute-start | bytes 2600 | tf_op jit(solution)/shard_map/ppermute | solution.py:31
  140.8 7.4 %collective-permute-start.20 = (f32[3,4,6,3]{3,1,2,0:T(4,128)S(1)}, f32[3,4,6,3]{3,1,2,0:T(4,128)S(1)}, u32[]{:S(2)}, u32[]{:S(2)}) collective-permute-start(f32[3,4,6,3]{3,1,2,0:T(4,128)S(1)} %get-tuple-element.1340), channel_id=1, source_target_pairs={{0,1},{1,2},{2,3},{4,5},{5,6},{6,7},{8,9},{9,10},{10,11},{12,13},{... | collective-permute-start | bytes 2600 | tf_op jit(solution)/shard_map/ppermute | solution.py:31
  (30 other events, 56.9 us)
where the time goes:
time: 151 us; the launch traced here: 150 us
  starting transfers between devices  52.9 us (35%)
  other arithmetic  47.9 us (32%)
  waiting for transfers between devices  27.1 us (18%)
  local copies, waits for them, and re-layouts  18.1 us (12%)
  between operations  4.13 us (3%)
    ppermute x13, starting transfers between devices, shifted(): lax.ppermute(value, axis, [(source, source + steps) for source in range(i...  32.2 us
    another operation x171, other arithmetic, pair_force(): return jnp.stack([magnitude * part for part in relative])  23.5 us
    ppermute x13, waiting for transfers between devices, shifted(): lax.ppermute(value, axis, [(source, source + steps) for source in range(i...  15.9 us
    ppermute x4, starting transfers between devices, with_halo(): lax.ppermute(lax.slice_in_dim(block, block.shape[dim] - width, None, axis...  15.6 us
    ppermute x4, waiting for transfers between devices, with_halo(): lax.ppermute(lax.slice_in_dim(block, 0, width, axis=dim), axis, backward)  10.6 us
    scatter-add x3, local copies, waits for them, and re-layouts, send_back(): interior = interior.at[:, :, :, rows_y - 3:].add(lower_rim)  8.35 us
    add x3, other arithmetic, on_device(): spread + jnp.pad(-force, ((0, 0), (step_x, 3 - step_x), (low_z, 3 - step_...  7.41 us
    ppermute x4, starting transfers between devices, with_halo(): lax.ppermute(lax.slice_in_dim(block, 0, width, axis=dim), axis, backward)  5.17 us
  transfers between devices with their start and end apart: 21, of which 10 were waited for; matrix products, arithmetic and copies ran while one was open for 8% of the time, Pallas kernels for 0%

commit v1 on v0

v1 whole, which is shorter than its diff:
```python
import functools
import math

import jax
import jax.numpy as jnp
from jax import lax
from jax.experimental import pallas as pl
from jax.experimental.pallas import tpu as pltpu
from jax.sharding import PartitionSpec as P

STEPS = 3
MATS = 8
time_step = 0.05
MESH = pl.DeviceIdType.MESH
DIRECTIONS = [(dx, dy) for dx in (-1, 0, 1) for dy in (-1, 0, 1) if (dx, dy) != (0, 0)]


def bond_offsets():
    chosen = []
    for step_x in range(0, 4):
        for step_z in range(-3, 4):
            for step_y in range(-3, 4):
                if step_x * step_x + step_z * step_z + step_y * step_y <= 9:
                    if step_x > 0 or (step_x == 0 and (step_z > 0 or (step_z == 0 and step_y > 0))):
                        chosen.append((step_x, step_z, step_y))
    return chosen


OFFSETS = bond_offsets()
SLOT = {}
for _sign in (1, -1):
    for _k in [k for k, d in enumerate(OFFSETS) if d[2] * _sign > 0]:
        SLOT[_k] = sum(1 for q in SLOT if OFFSETS[q][2] * _sign > 0)
SHELL = sorted(
    [(k, True, d) for k, d in enumerate(OFFSETS)]
    + [(k, False, (-d[0], -d[1], -d[2])) for k, d in enumerate(OFFSETS)],
    key=lambda item: item[2],
)
GROUPS = {
    a: [k for k, d in enumerate(OFFSETS) if d[0] == a] for a in sorted({d[0] for d in OFFSETS}) if a > 0
}


def kernel(
    shape,
    disp_in, vel_in, lab_in, mask_in, stiff, crit,
    disp_out, vel_out,
    ext, edge_send, edge_land, mat_ext, mat_send, mat_land,
    mask_x1, mask_x2, mask_x3, mask_ext, pack_send, pack_land,
    moved, mat_moved, gain, spread, vel,
    send_sem, recv_sem, mat_ssem, mat_rsem, mx_ssem, mx_rsem, pk_ssem, pk_rsem,
):
    nx, nz, ny = shape
    rows = nx * nz
    size_x, size_y = lax.axis_size("wx"), lax.axis_size("ny")
    my_x, my_y = lax.axis_index("wx"), lax.axis_index("ny")
    lane = lax.broadcasted_iota(jnp.int32, (rows, ny), 1)
    row = lax.broadcasted_iota(jnp.int32, (rows, ny), 0)
    depth = row % nz
    mask_x = (mask_x1, mask_x2, mask_x3)

    def roll(value, shift):
        shift = shift % ny
        return value if shift == 0 else pltpu.roll(value, shift, 1)

    def exists(dx, dy):
        ok = my_x >= 0
        if dx != 0:
            ok = (my_x + dx >= 0) & (my_x + dx < size_x)
        if dy != 0:
            ok = ok & (my_y + dy >= 0) & (my_y + dy < size_y)
        return ok

    ext[...] = jnp.zeros_like(ext)
    edge_land[...] = jnp.zeros_like(edge_land)
    mat_ext[...] = jnp.zeros_like(mat_ext)
    mat_land[...] = jnp.zeros_like(mat_land)
    pack_land[...] = jnp.zeros_like(pack_land)
    for ref in mask_x:
        ref[...] = jnp.zeros_like(ref)

    barrier = pltpu.get_barrier_semaphore()
    for dx, dy in DIRECTIONS:
        @pl.when(exists(dx, dy))
        def _(dx=dx, dy=dy):
            pl.semaphore_signal(
                barrier, inc=1, device_id=(my_x + dx, my_y + dy), device_id_type=MESH
            )

    def pack_edges(fields, target):
        up = jnp.zeros((rows, ny), jnp.float32)
        down = jnp.zeros((rows, ny), jnp.float32)
        for f, value in enumerate(fields):
            up = jnp.where(lane // 4 == ny // 4 - 1 - f, roll(value, -4 * f), up)
            down = jnp.where(lane // 4 == f, roll(value, 4 * f), down)
        target[0] = up
        target[1] = down

    def halo_copies(whole, sent, land, ssem, rsem):
        copies = []
        for index, (dx, dy) in enumerate(DIRECTIONS):
            place = pl.ds((1 - dx) * rows, rows)
            if dy == 0:
                source = whole.at[:, pl.ds(rows, rows), :]
                target = whole.at[:, place, :]
            else:
                side = 0 if dy > 0 else 1
                source = sent.at[side]
                target = land.at[side, place, :]
            copy = pltpu.make_async_remote_copy(
                src_ref=source, dst_ref=target, send_sem=ssem.at[index], recv_sem=rsem.at[index],
                device_id=(my_x + dx, my_y + dy), device_id_type=MESH,
            )
            copies.append((dx, dy, copy))
        return copies

    def mask_copies():
        copies = []
        for number, (a, members) in enumerate(GROUPS.items()):
            copies.append((1, 0, pltpu.make_async_remote_copy(
                src_ref=mask_in.at[pl.ds(members[0], len(members)), pl.ds(nx - a, a)],
                dst_ref=mask_x[number],
                send_sem=mx_ssem.at[number], recv_sem=mx_rsem.at[number],
                device_id=(my_x + 1, my_y), device_id_type=MESH,
            )))
        return copies

    def pack_copies():
        copies = []
        for index, (dx, dy) in enumerate([(0, 1), (0, -1), (1, 1), (1, -1)]):
            side = 0 if dy > 0 else 1
            copies.append((dx, dy, pltpu.make_async_remote_copy(
                src_ref=pack_send.at[side],
                dst_ref=pack_land.at[side, pl.ds((1 - dx) * rows, rows), :],
                send_sem=pk_ssem.at[index], recv_sem=pk_rsem.at[index],
                device_id=(my_x + dx, my_y + dy), device_id_type=MESH,
            )))
        return copies

    def start(copies):
        for dx, dy, copy in copies:
            pl.when(exists(dx, dy))(copy.start)

    def arrive(copies):
        for dx, dy, copy in copies:
            pl.when(exists(-dx, -dy))(copy.wait_recv)

    def leave(copies):
        for dx, dy, copy in copies:
            pl.when(exists(dx, dy))(copy.wait_send)

    def step_copies(s):
        return halo_copies(ext.at[s], edge_send.at[s], edge_land.at[s], send_sem.at[s], recv_sem.at[s])

    mat_copies = halo_copies(mat_ext, mat_send, mat_land, mat_ssem, mat_rsem)

    for x in range(nx):
        at = pl.ds(rows + x * nz, nz)
        for f in range(3):
            ext[0, f, at, :] = disp_in[f, x]
            vel[f, pl.ds(x * nz, nz), :] = vel_in[f, x]
        labels = lab_in[x]
        modulus = jnp.zeros(labels.shape, jnp.float32)
        limit = jnp.zeros(labels.shape, jnp.float32)
        for material in range(MATS):
            matches = labels == material
            modulus = jnp.where(matches, stiff[material], modulus)
            limit = jnp.where(matches, crit[material], limit)
        mat_ext[0, at, :] = modulus
        mat_ext[1, at, :] = limit
    own = pl.ds(rows, rows)
    pack_edges([mat_ext[f, own, :] for f in range(2)], mat_send)
    pack_edges([ext[0, f, own, :] for f in range(3)], edge_send.at[0])

    neighbours = lax.select(my_x > 0, 1, 0) + lax.select(my_x < size_x - 1, 1, 0) + 1
    neighbours = neighbours * (lax.select(my_y > 0, 1, 0) + lax.select(my_y < size_y - 1, 1, 0) + 1) - 1
    pl.semaphore_wait(barrier, neighbours)
    start(mat_copies)
    start(mask_copies())
    start(step_copies(0))

    up = jnp.zeros((rows, ny), jnp.float32)
    down = jnp.zeros((rows, ny), jnp.float32)
    for k, d in enumerate(OFFSETS):
        for x in range(nx):
            mask_ext[k, pl.ds(rows + x * nz, nz), :] = mask_in[k, x].astype(jnp.float32)
        c = d[2]
        if c > 0:
            value = mask_ext[k, own, :]
            up = jnp.where(lane // 4 == SLOT[k], roll(value, c + 4 * SLOT[k]), up)
        elif c < 0:
            value = mask_ext[k, own, :]
            down = jnp.where(lane // 4 == ny // 4 - 1 - SLOT[k], roll(value, c - 4 * SLOT[k]), down)
    pack_send[0] = up
    pack_send[1] = down
    start(pack_copies())

    def shift_fields(source, land, target, count, add_step):
        full = 3 * rows
        lanes = lax.broadcasted_iota(jnp.int32, (full, ny), 1)
        for f in range(count):
            value = source[f]
            high = roll(land[1], -4 * f)
            low = roll(land[0], 4 * f)
            for c in range(-3, 4):
                moved_value = value
                if c > 0:
                    moved_value = roll(jnp.where(lanes < c, high, value), -c)
                elif c < 0:
                    moved_value = roll(jnp.where(lanes >= ny + c, low, value), -c)
                if add_step and f == 2 and c != 0:
                    moved_value = moved_value + float(c)
                target[c + 3, f] = moved_value

    arrive(mat_copies)
    shift_fields(mat_ext, mat_land, mat_moved, 2, False)

    def inside_depth(b):
        return jnp.where((depth + b >= 0) & (depth + b < nz), 1.0, 0.0).astype(jnp.float32)

    def coefficients(number, offset, live):
        a, b, c = offset
        length = math.sqrt(a * a + b * b + c * c)
        at = pl.ds(rows + nz * a + b, rows)
        here, there = mat_ext[0, own, :], mat_moved[c + 3, 0, at, :]
        limit = mat_ext[1, own, :] + mat_moved[c + 3, 1, at, :]
        square = limit * limit * (0.25 * length * length)
        if b != 0:
            live = live * inside_depth(b)
        gain[number] = (here * there) / (here + there) * (square * (2.0 / length**3)) * live
        spread[number] = square

    for number, (k, forward, offset) in enumerate(SHELL):
        if forward:
            coefficients(number, offset, mask_ext[k, own, :])

    arrive(mask_copies())
    arrive(pack_copies())
    for number, (a, members) in enumerate(GROUPS.items()):
        for place, k in enumerate(members):
            mask_ext[k, pl.ds(0, rows), :] = jnp.zeros((rows, ny), jnp.float32)
            for x in range(a):
                mask_ext[k, pl.ds((nx - a + x) * nz, nz), :] = mask_x[number][place, x].astype(jnp.float32)
    for k in range(GROUPS[1][0]):
        mask_ext[k, pl.ds(0, rows), :] = jnp.zeros((rows, ny), jnp.float32)
    for number, (k, forward, offset) in enumerate(SHELL):
        if not forward:
            a, b, c = OFFSETS[k]
            at = pl.ds(rows - nz * a - b, rows)
            live = roll(mask_ext[k, at, :], c)
            if c > 0:
                live = jnp.where(lane < c, roll(pack_land[0, at, :], -4 * SLOT[k]), live)
            elif c < 0:
                live = jnp.where(lane >= ny + c, roll(pack_land[1, at, :], 4 * SLOT[k]), live)
            coefficients(number, offset, live)

    def one_step(s, carry):
        arrive(step_copies(s))
        shift_fields(ext.at[s], edge_land.at[s], moved, 3, True)
        here = [ext[s, f, own, :] for f in range(3)]
        force = [jnp.zeros((rows, ny), jnp.float32) for _ in range(3)]
        for number, (k, forward, offset) in enumerate(SHELL):
            a, b, c = offset
            length = math.sqrt(a * a + b * b + c * c)
            at = pl.ds(rows + nz * a + b, rows)
            e = [
                moved[c + 3, 0, at, :] - (here[0] - float(a)),
                moved[c + 3, 1, at, :] - (here[1] - float(b)),
                moved[c + 3, 2, at, :] - here[2],
            ]
            square = jnp.maximum(e[0] * e[0] + e[1] * e[1] + e[2] * e[2], 1e-30)
            t = square * lax.rsqrt(square) - length
            magnitude = gain[number] * t / (spread[number] + t * t)
            force = [force[f] + magnitude * e[f] for f in range(3)]
        fresh = []
        for f in range(3):
            velocity = vel[f] + time_step * force[f]
            vel[f] = velocity
            fresh.append(here[f] + time_step * velocity)

        @pl.when(s < STEPS - 1)
        def _():
            for f in range(3):
                ext[s + 1, f, own, :] = fresh[f]
            pack_edges(fresh, edge_send.at[s + 1])
            start(step_copies(s + 1))

        @pl.when(s == STEPS - 1)
        def _():
            for f in range(3):
                moved[3, f, pl.ds(0, rows), :] = fresh[f]
        return carry

    lax.fori_loop(0, STEPS, one_step, 0)
    for f in range(3):
        for x in range(nx):
            disp_out[f, x] = moved[3, f, pl.ds(x * nz, nz), :]
            vel_out[f, x] = vel[f, pl.ds(x * nz, nz), :]

    leave(mat_copies)
    leave(mask_copies())
    leave(pack_copies())

    def drain(s, carry):
        leave(step_copies(s))
        return carry

    lax.fori_loop(0, STEPS, drain, 0)


def on_device(displacement, velocity, labels, bond_mask, stiffness, critical):
    nx, nz, ny = labels.shape
    rows = nx * nz
    count = len(SHELL)
    f32 = jnp.float32
    vmem, smem = pl.BlockSpec(memory_space=pltpu.VMEM), pl.BlockSpec(memory_space=pltpu.SMEM)
    dma = pltpu.SemaphoreType.DMA
    return pl.pallas_call(
        functools.partial(kernel, (nx, nz, ny)),
        out_shape=[jax.ShapeDtypeStruct(displacement.shape, f32)] * 2,
        in_specs=[vmem] * 4 + [smem] * 2,
        out_specs=[vmem] * 2,
        scratch_shapes=[
            pltpu.VMEM((STEPS, 3, 3 * rows, ny), f32),
            pltpu.VMEM((STEPS, 2, rows, ny), f32),
            pltpu.VMEM((STEPS, 2, 3 * rows, ny), f32),
            pltpu.VMEM((2, 3 * rows, ny), f32),
            pltpu.VMEM((2, rows, ny), f32),
            pltpu.VMEM((2, 3 * rows, ny), f32),
            pltpu.VMEM((len(GROUPS[1]), 1, nz, ny), jnp.int32),
            pltpu.VMEM((len(GROUPS[2]), 2, nz, ny), jnp.int32),
            pltpu.VMEM((len(GROUPS[3]), 3, nz, ny), jnp.int32),
            pltpu.VMEM((len(OFFSETS), 2 * rows, ny), f32),
            pltpu.VMEM((2, rows, ny), f32),
            pltpu.VMEM((2, 2 * rows, ny), f32),
            pltpu.VMEM((7, 3, 3 * rows, ny), f32),
            pltpu.VMEM((7, 2, 3 * rows, ny), f32),
            pltpu.VMEM((count, rows, ny), f32),
            pltpu.VMEM((count, rows, ny), f32),
            pltpu.VMEM((3, rows, ny), f32),
            dma((STEPS, 8)), dma((STEPS, 8)), dma((8,)), dma((8,)),
            dma((3,)), dma((3,)), dma((4,)), dma((4,)),
        ],
        compiler_params=pltpu.CompilerParams(
            collective_id=0, has_side_effects=True, vmem_limit_bytes=40 * 1024 * 1024
        ),
        name="peridynamics",
    )(displacement, velocity, labels, bond_mask, stiffness, critical)


def solution(mesh):
    in_specs = (
        P(None, "wx", None, "ny"),
        P(None, "wx", None, "ny"),
        P("wx", None, "ny"),
        P(None, "wx", None, "ny"),
        P(),
        P(),
    )
    out_specs = (P(None, "wx", None, "ny"), P(None, "wx", None, "ny"))
    return jax.shard_map(
        on_device, mesh=mesh, in_specs=in_specs, out_specs=out_specs, check_vma=False
    )
```

time: 151 us -> 28.2 us (0.19)
  starting transfers between devices: 52.9 us -> 0 us
  other arithmetic: 47.9 us -> 0 us
  waiting for transfers between devices: 27.1 us -> 0 us
  Pallas kernels: 0 us -> 23.2 us
  local copies, waits for them, and re-layouts: 18.1 us -> 4.04 us
  between operations: 4.13 us -> 0.69 us
    ppermute x21 -> x0, starting transfers between devices: 52.9 us -> none  [the longest x13 32.2 us: shifted(): lax.ppermute(value, axis, [(source, source + steps) for source in range(i...]
    ppermute x21 -> x0, waiting for transfers between devices: 27.1 us -> none  [the longest x13 15.9 us: shifted(): lax.ppermute(value, axis, [(source, source + steps) for source in range(i...]
    another operation x172 -> x0, other arithmetic: 23.6 us -> none  [the longest x171 23.5 us: pair_force(): return jnp.stack([magnitude * part for part in relative])]
    pallas_call x0 -> x1, Pallas kernels: none -> 23.2 us  [on_device(): pl.pallas_call(functools.partial(kernel, (nx, nz, ny)), out_shape=[jax.Sh...]
    add x15 -> x0, other arithmetic: 10.7 us -> none  [the longest x3 7.41 us: on_device(): spread + jnp.pad(-force, ((0, 0), (step_x, 3 - step_x), (low_z, 3 - step_...]
    scatter-add x9 -> x0, local copies, waits for them, and re-layouts: 10.2 us -> none  [the longest x3 8.35 us: send_back(): interior = interior.at[:, :, :, rows_y - 3:].add(lower_rim)]
    select_n x2 -> x0, other arithmetic: 9.94 us -> none  [the longest x1 5.01 us: node_material(): strain_limit = jnp.where(matches, critical[material], strain_limit)]
    slice x17 -> x0, local copies, waits for them, and re-layouts: 3.15 us -> none  [the longest x1 1.63 us: node_material(): modulus = jnp.where(matches, stiffness[material], modulus)]
  transfers between devices with their start and end apart: 21 -> 0, of which waited for: 10 -> 0; matrix products, arithmetic and copies ran while one was open for 8% -> 0% of each run, Pallas kernels for 0% -> 0%
where the time goes in v1:
time: 28.2 us; the launch traced here: 27.9 us
  Pallas kernels  23.2 us (82%)
  local copies, waits for them, and re-layouts  4.04 us (14%)
  between operations  0.69 us (2%)
    pallas_call x1, Pallas kernels, on_device(): pl.pallas_call(functools.partial(kernel, (nx, nz, ny)), out_shape=[jax.Sh...  23.2 us
    unnamed x10, local copies, waits for them, and re-layouts  2.79 us
    pallas_call x2, local copies, waits for them, and re-layouts, on_device(): pl.pallas_call(functools.partial(kernel, (nx, nz, ny)), out_shape=[jax.Sh...  1.25 us

profile of v1, /device:TPU:4, one launch (start us, length us, event | category | flops | bytes accessed | tf_op | source)
XLA Modules:
  0.0 27.9 jit_solution(12374652539396318875)
XLA Ops:
  0.6 0.7 %copy.10.lab_in = s32[4,6,128]{2,1,0:T(8,128)S(1)} copy(s32[4,6,128]{2,0,1:T(4,128)} %param.8) | data formatting | bytes 24576 | tf_op args[2]
  1.3 0.0 copy-start.2
  1.3 0.8 %copy.8.disp_in = f32[3,4,6,128]{3,2,1,0:T(8,128)S(1)} copy(f32[3,4,6,128]{3,1,2,0:T(4,128)} %param.6) | data formatting | bytes 73728 | tf_op args[0]
  2.1 0.0 copy-done.2
  2.1 0.0 copy-start
  2.2 0.0 copy-start.1
  2.2 1.3 %copy.11.mask_in = s32[61,4,6,128]{3,2,1,0:T(8,128)S(1)} copy(s32[61,4,6,128]{3,1,2,0:T(4,128)} %param.9) | data formatting | bytes 1499136 | tf_op args[3]
  3.4 0.0 copy-done
  3.5 0.0 copy-done.1
  3.5 23.2 %peridynamics.1 = (f32[3,4,6,128]{3,2,1,0:T(8,128)S(1)}, f32[3,4,6,128]{3,2,1,0:T(8,128)S(1)}) custom-call(f32[3,4,6,128]{3,2,1,0:T(8,128)S(1)} %copy.8.disp_in, f32[3,4,6,128]{3,2,1,0:T(8,128)S(1)} %copy.9.vel_in, s32[4,6,128]{2,1,0:T(8,128)S(1)} %copy.10.lab_in, s32[61,4,6,128]{3,2,1,0:T(8,128)S(1)} %copy.11.mask_in, f32[8]{0:T(128)S(1)} %copy-done, ...), custom_call_target="tpu_custom_call" | custom-call | tf_op jit(solution)/shard_map/peridynamics/pallas_call | solution.py:318
  26.7 0.6 %copy.12 = f32[3,4,6,128]{3,1,2,0:T(4,128)} copy(f32[3,4,6,128]{3,2,1,0:T(8,128)S(1)} %get-tuple-element.2) | data formatting | bytes 73728 | tf_op jit(solution)/shard_map/peridynamics/pallas_call | solution.py:318
  27.3 0.6 %copy.13 = f32[3,4,6,128]{3,1,2,0:T(4,128)} copy(f32[3,4,6,128]{3,2,1,0:T(8,128)S(1)} %get-tuple-element.3) | data formatting | bytes 73728 | tf_op jit(solution)/shard_map/peridynamics/pallas_call | solution.py:318
  (1 shorter events, 0.0 us)
Async XLA Ops:
  1.3 0.8 %copy-start.2 = (f32[3,4,6,128]{3,1,2,0:T(4,128)S(1)}, f32[3,4,6,128]{3,1,2,0:T(4,128)}, u32[]{:S(2)}) copy-start(f32[3,4,6,128]{3,1,2,0:T(4,128)} %param.7) | copy-start | bytes 110596
  2.1 1.3 %copy-start = (f32[8]{0:T(128)S(1)}, f32[8]{0:T(128)}, u32[]{:S(2)}) copy-start(f32[8]{0:T(128)} %stiff.1) | copy-start | bytes 100
  2.2 1.3 %copy-start.1 = (f32[8]{0:T(128)S(1)}, f32[8]{0:T(128)}, u32[]{:S(2)}) copy-start(f32[8]{0:T(128)} %crit.1) | copy-start | bytes 100

commit v2 on v1

--- a/solution.py
+++ b/solution.py
@@ -36,9 +36,7 @@
     + [(k, False, (-d[0], -d[1], -d[2])) for k, d in enumerate(OFFSETS)],
     key=lambda item: item[2],
 )
-GROUPS = {
-    a: [k for k, d in enumerate(OFFSETS) if d[0] == a] for a in sorted({d[0] for d in OFFSETS}) if a > 0
-}
+FLAT = sum(1 for d in OFFSETS if d[0] == 0)
 
 
 def kernel(
@@ -46,7 +44,7 @@
     disp_in, vel_in, lab_in, mask_in, stiff, crit,
     disp_out, vel_out,
     ext, edge_send, edge_land, mat_ext, mat_send, mat_land,
-    mask_x1, mask_x2, mask_x3, mask_ext, pack_send, pack_land,
+    mask_send, mask_land, mask_ext, pack_send, pack_land,
     moved, mat_moved, gain, spread, vel,
     send_sem, recv_sem, mat_ssem, mat_rsem, mx_ssem, mx_rsem, pk_ssem, pk_rsem,
 ):
@@ -57,7 +55,9 @@
     lane = lax.broadcasted_iota(jnp.int32, (rows, ny), 1)
     row = lax.broadcasted_iota(jnp.int32, (rows, ny), 0)
     depth = row % nz
-    mask_x = (mask_x1, mask_x2, mask_x3)
+
+    def layer(x):
+        return pl.ds(x, nz, stride=nx)
 
     def roll(value, shift):
         shift = shift % ny
@@ -76,8 +76,7 @@
     mat_ext[...] = jnp.zeros_like(mat_ext)
     mat_land[...] = jnp.zeros_like(mat_land)
     pack_land[...] = jnp.zeros_like(pack_land)
-    for ref in mask_x:
-        ref[...] = jnp.zeros_like(ref)
+    mask_land[...] = jnp.zeros_like(mask_land)
 
     barrier = pltpu.get_barrier_semaphore()
     for dx, dy in DIRECTIONS:
@@ -115,15 +114,10 @@
         return copies
 
     def mask_copies():
-        copies = []
-        for number, (a, members) in enumerate(GROUPS.items()):
-            copies.append((1, 0, pltpu.make_async_remote_copy(
-                src_ref=mask_in.at[pl.ds(members[0], len(members)), pl.ds(nx - a, a)],
-                dst_ref=mask_x[number],
-                send_sem=mx_ssem.at[number], recv_sem=mx_rsem.at[number],
-                device_id=(my_x + 1, my_y), device_id_type=MESH,
-            )))
-        return copies
+        return [(1, 0, pltpu.make_async_remote_copy(
+            src_ref=mask_send, dst_ref=mask_land, send_sem=mx_ssem.at[0], recv_sem=mx_rsem.at[0],
+            device_id=(my_x + 1, my_y), device_id_type=MESH,
+        ))]
 
     def pack_copies():
         copies = []
@@ -157,9 +151,9 @@
     for x in range(nx):
         at = pl.ds(rows + x * nz, nz)
         for f in range(3):
-            ext[0, f, at, :] = disp_in[f, x]
-            vel[f, pl.ds(x * nz, nz), :] = vel_in[f, x]
-        labels = lab_in[x]
+            ext[0, f, at, :] = disp_in[f, layer(x), :]
+            vel[f, pl.ds(x * nz, nz), :] = vel_in[f, layer(x), :]
+        labels = lab_in[layer(x), :]
         modulus = jnp.zeros(labels.shape, jnp.float32)
         limit = jnp.zeros(labels.shape, jnp.float32)
         for material in range(MATS):
@@ -176,14 +170,21 @@
     neighbours = neighbours * (lax.select(my_y > 0, 1, 0) + lax.select(my_y < size_y - 1, 1, 0) + 1) - 1
     pl.semaphore_wait(barrier, neighbours)
     start(mat_copies)
-    start(mask_copies())
     start(step_copies(0))
+
+    def mask_row(k, x):
+        return nz * (sum(OFFSETS[q][0] for q in range(k)) + x)
 
     up = jnp.zeros((rows, ny), jnp.float32)
     down = jnp.zeros((rows, ny), jnp.float32)
     for k, d in enumerate(OFFSETS):
         for x in range(nx):
-            mask_ext[k, pl.ds(rows + x * nz, nz), :] = mask_in[k, x].astype(jnp.float32)
+            value = mask_in[k, layer(x), :].astype(jnp.float32)
+            mask_ext[k, pl.ds(rows + x * nz, nz), :] = value
+            if x >= nx - d[0]:
+                mask_send[pl.ds(mask_row(k, x - (nx - d[0])), nz), :] = value
+    start(mask_copies())
+    for k, d in enumerate(OFFSETS):
         c = d[2]
         if c > 0:
             value = mask_ext[k, own, :]
@@ -236,12 +237,11 @@
 
     arrive(mask_copies())
     arrive(pack_copies())
-    for number, (a, members) in enumerate(GROUPS.items()):
-        for place, k in enumerate(members):
-            mask_ext[k, pl.ds(0, rows), :] = jnp.zeros((rows, ny), jnp.float32)
-            for x in range(a):
-                mask_ext[k, pl.ds((nx - a + x) * nz, nz), :] = mask_x[number][place, x].astype(jnp.float32)
-    for k in range(GROUPS[1][0]):
+    for k in range(FLAT, len(OFFSETS)):
+        a = OFFSETS[k][0]
+        mask_ext[k, pl.ds(0, rows), :] = jnp.zeros((rows, ny), jnp.float32)
+        mask_ext[k, pl.ds((nx - a) * nz, a * nz), :] = mask_land[pl.ds(mask_row(k, 0), a * nz), :]
+    for k in range(FLAT):
         mask_ext[k, pl.ds(0, rows), :] = jnp.zeros((rows, ny), jnp.float32)
     for number, (k, forward, offset) in enumerate(SHELL):
         if not forward:
@@ -294,8 +294,8 @@
     lax.fori_loop(0, STEPS, one_step, 0)
     for f in range(3):
         for x in range(nx):
-            disp_out[f, x] = moved[3, f, pl.ds(x * nz, nz), :]
-            vel_out[f, x] = vel[f, pl.ds(x * nz, nz), :]
+            disp_out[f, layer(x), :] = moved[3, f, pl.ds(x * nz, nz), :]
+            vel_out[f, layer(x), :] = vel[f, pl.ds(x * nz, nz), :]
 
     leave(mat_copies)
     leave(mask_copies())
@@ -312,12 +312,19 @@
     nx, nz, ny = labels.shape
     rows = nx * nz
     count = len(SHELL)
+    edge_rows = -(-nz * sum(d[0] for d in OFFSETS) // 8) * 8
+
+    def by_depth(value):
+        lead = value.shape[:-3]
+        order = tuple(range(len(lead))) + tuple(len(lead) + i for i in (1, 0, 2))
+        return value.transpose(order).reshape(lead + (rows, ny))
+
     f32 = jnp.float32
     vmem, smem = pl.BlockSpec(memory_space=pltpu.VMEM), pl.BlockSpec(memory_space=pltpu.SMEM)
     dma = pltpu.SemaphoreType.DMA
-    return pl.pallas_call(
+    results = pl.pallas_call(
         functools.partial(kernel, (nx, nz, ny)),
-        out_shape=[jax.ShapeDtypeStruct(displacement.shape, f32)] * 2,
+        out_shape=[jax.ShapeDtypeStruct((3, rows, ny), f32)] * 2,
         in_specs=[vmem] * 4 + [smem] * 2,
         out_specs=[vmem] * 2,
         scratch_shapes=[
@@ -327,9 +334,8 @@
             pltpu.VMEM((2, 3 * rows, ny), f32),
             pltpu.VMEM((2, rows, ny), f32),
             pltpu.VMEM((2, 3 * rows, ny), f32),
-            pltpu.VMEM((len(GROUPS[1]), 1, nz, ny), jnp.int32),
-            pltpu.VMEM((len(GROUPS[2]), 2, nz, ny), jnp.int32),
-            pltpu.VMEM((len(GROUPS[3]), 3, nz, ny), jnp.int32),
+            pltpu.VMEM((edge_rows, ny), f32),
+            pltpu.VMEM((edge_rows, ny), f32),
             pltpu.VMEM((len(OFFSETS), 2 * rows, ny), f32),
             pltpu.VMEM((2, rows, ny), f32),
             pltpu.VMEM((2, 2 * rows, ny), f32),
@@ -339,13 +345,17 @@
             pltpu.VMEM((count, rows, ny), f32),
             pltpu.VMEM((3, rows, ny), f32),
             dma((STEPS, 8)), dma((STEPS, 8)), dma((8,)), dma((8,)),
-            dma((3,)), dma((3,)), dma((4,)), dma((4,)),
+            dma((1,)), dma((1,)), dma((4,)), dma((4,)),
         ],
         compiler_params=pltpu.CompilerParams(
             collective_id=0, has_side_effects=True, vmem_limit_bytes=40 * 1024 * 1024
         ),
         name="peridynamics",
-    )(displacement, velocity, labels, bond_mask, stiffness, critical)
+    )(
+        by_depth(displacement), by_depth(velocity), by_depth(labels), by_depth(bond_mask),
+        stiffness, critical,
+    )
+    return tuple(value.reshape(3, nz, nx, ny).transpose(0, 2, 1, 3) for value in results)
 
 
 def solution(mesh):

time: 28.2 us -> 29.8 us (1.057)
  local copies, waits for them, and re-layouts: 4.04 us -> 5.25 us
  Pallas kernels: 23.2 us -> 23.5 us
    unnamed x10 -> x14, local copies, waits for them, and re-layouts: 2.79 us -> 5.25 us
    pallas_call x2 -> x0, local copies, waits for them, and re-layouts: 1.25 us -> none  [on_device(): pl.pallas_call(functools.partial(kernel, (nx, nz, ny)), out_shape=[jax.Sh...]
    pallas_call x1, Pallas kernels: 23.2 us -> 23.5 us  [on_device(): pl.pallas_call(functools.partial(kernel, (nx, nz, ny)), out_shape=[jax.Sh...]
where the time goes in v2:
time: 29.8 us; the launch traced here: 29.4 us
  Pallas kernels  23.5 us (79%)
  local copies, waits for them, and re-layouts  5.25 us (18%)
  between operations  0.66 us (2%)
    pallas_call x1, Pallas kernels, on_device(): pl.pallas_call(functools.partial(kernel, (nx, nz, ny)), out_shape=[jax.Sh...  23.5 us
    unnamed x14, local copies, waits for them, and re-layouts  5.25 us

profile of v2, /device:TPU:4, one launch (start us, length us, event | category | flops | bytes accessed | tf_op | source)
XLA Modules:
  0.0 29.4 jit_solution(18039320711951422776)
XLA Ops:
  0.6 0.0 copy-start.4
  0.6 0.0 copy-start.5
  0.7 0.6 %copy-done.4 = f32[8]{0:T(128)S(1)} copy-done((f32[8]{0:T(128)S(1)}, f32[8]{0:T(128)}, u32[]{:S(2)}) %copy-start.4) | copy-done | bytes 56
  1.3 0.0 copy-done.5
  1.3 0.0 copy-start
  1.3 1.1 %copy-done = s32[61,4,6,128]{3,1,2,0:T(4,128)S(1)} copy-done((s32[61,4,6,128]{3,1,2,0:T(4,128)S(1)}, s32[61,4,6,128]{3,1,2,0:T(4,128)}, u32[]{:S(2)}) %copy-start) | copy-done | bytes 749592
  2.4 0.0 copy-start.1
  2.4 0.8 %copy-done.1 = f32[3,4,6,128]{3,1,2,0:T(4,128)S(1)} copy-done((f32[3,4,6,128]{3,1,2,0:T(4,128)S(1)}, f32[3,4,6,128]{3,1,2,0:T(4,128)}, u32[]{:S(2)}) %copy-start.1) | copy-done | bytes 36888
  3.2 0.0 copy-start.2
  3.2 0.8 %copy-done.2 = f32[3,4,6,128]{3,1,2,0:T(4,128)S(1)} copy-done((f32[3,4,6,128]{3,1,2,0:T(4,128)S(1)}, f32[3,4,6,128]{3,1,2,0:T(4,128)}, u32[]{:S(2)}) %copy-start.2) | copy-done | bytes 36888
  4.0 0.0 copy-start.3
  4.0 0.7 %copy-done.3 = s32[4,6,128]{2,0,1:T(4,128)S(1)} copy-done((s32[4,6,128]{2,0,1:T(4,128)S(1)}, s32[4,6,128]{2,0,1:T(4,128)}, u32[]{:S(2)}) %copy-start.3) | copy-done | bytes 12312
  4.7 23.5 %peridynamics.1 = (f32[3,24,128]{2,1,0:T(8,128)S(1)}, f32[3,24,128]{2,1,0:T(8,128)S(1)}) custom-call(f32[3,24,128]{2,1,0:T(8,128)S(1)} %bitcast.19, f32[3,24,128]{2,1,0:T(8,128)S(1)} %bitcast.20, s32[24,128]{1,0:T(8,128)S(1)} %bitcast.23, s32[61,24,128]{2,1,0:T(8,128)S(1)} %bitcast.18, f32[8]{0:T(128)S(1)} %copy-done.4, f32[8]{0:T(128)S(1)} %copy-done.5), custom_call_target="tpu_custom_call" | custom-call | tf_op jit(solution)/shard_map/peridynamics/pallas_call | solution.py:325
  28.2 0.6 %copy.10 = f32[3,4,6,128]{3,1,2,0:T(4,128)} copy(f32[3,4,6,128]{3,1,2,0:T(4,128)S(1)} %bitcast.22) | data formatting | bytes 73728
  28.8 0.6 %copy.11 = f32[3,4,6,128]{3,1,2,0:T(4,128)} copy(f32[3,4,6,128]{3,1,2,0:T(4,128)S(1)} %bitcast.21) | data formatting | bytes 73728
Async XLA Ops:
  0.6 0.7 %copy-start.4 = (f32[8]{0:T(128)S(1)}, f32[8]{0:T(128)}, u32[]{:S(2)}) copy-start(f32[8]{0:T(128)} %stiff.1) | copy-start | bytes 100
  0.6 0.7 %copy-start.5 = (f32[8]{0:T(128)S(1)}, f32[8]{0:T(128)}, u32[]{:S(2)}) copy-start(f32[8]{0:T(128)} %crit.1) | copy-start | bytes 100
  1.3 1.1 %copy-start = (s32[61,4,6,128]{3,1,2,0:T(4,128)S(1)}, s32[61,4,6,128]{3,1,2,0:T(4,128)}, u32[]{:S(2)}) copy-start(s32[61,4,6,128]{3,1,2,0:T(4,128)} %param.9) | copy-start | bytes 2248708
  2.4 0.8 %copy-start.1 = (f32[3,4,6,128]{3,1,2,0:T(4,128)S(1)}, f32[3,4,6,128]{3,1,2,0:T(4,128)}, u32[]{:S(2)}) copy-start(f32[3,4,6,128]{3,1,2,0:T(4,128)} %param.6) | copy-start | bytes 110596
  3.2 0.8 %copy-start.2 = (f32[3,4,6,128]{3,1,2,0:T(4,128)S(1)}, f32[3,4,6,128]{3,1,2,0:T(4,128)}, u32[]{:S(2)}) copy-start(f32[3,4,6,128]{3,1,2,0:T(4,128)} %param.7) | copy-start | bytes 110596
  4.0 0.7 %copy-start.3 = (s32[4,6,128]{2,0,1:T(4,128)S(1)}, s32[4,6,128]{2,0,1:T(4,128)}, u32[]{:S(2)}) copy-start(s32[4,6,128]{2,0,1:T(4,128)} %param.8) | copy-start | bytes 36868

commit v3 on v2

--- a/solution.py
+++ b/solution.py
@@ -41,8 +41,9 @@
 
 def kernel(
     shape,
-    disp_in, vel_in, lab_in, mask_in, stiff, crit,
+    disp_far, vel_far, lab_far, mask_far, stiff, crit,
     disp_out, vel_out,
+    disp_in, vel_in, lab_in, mask_in, in_sem,
     ext, edge_send, edge_land, mat_ext, mat_send, mat_land,
     mask_send, mask_land, mask_ext, pack_send, pack_land,
     moved, mat_moved, gain, spread, vel,
@@ -70,6 +71,15 @@
         if dy != 0:
             ok = ok & (my_y + dy >= 0) & (my_y + dy < size_y)
         return ok
+
+    reads = [
+        pltpu.make_async_copy(source, target, in_sem.at[number])
+        for number, (source, target) in enumerate(
+            [(lab_far, lab_in), (disp_far, disp_in), (vel_far, vel_in), (mask_far, mask_in)]
+        )
+    ]
+    for read in reads:
+        read.start()
 
     ext[...] = jnp.zeros_like(ext)
     edge_land[...] = jnp.zeros_like(edge_land)
@@ -148,6 +158,8 @@
 
     mat_copies = halo_copies(mat_ext, mat_send, mat_land, mat_ssem, mat_rsem)
 
+    for read in reads[:3]:
+        read.wait()
     for x in range(nx):
         at = pl.ds(rows + x * nz, nz)
         for f in range(3):
@@ -171,6 +183,8 @@
     pl.semaphore_wait(barrier, neighbours)
     start(mat_copies)
     start(step_copies(0))
+
+    reads[3].wait()
 
     def mask_row(k, x):
         return nz * (sum(OFFSETS[q][0] for q in range(k)) + x)
@@ -325,9 +339,14 @@
     results = pl.pallas_call(
         functools.partial(kernel, (nx, nz, ny)),
         out_shape=[jax.ShapeDtypeStruct((3, rows, ny), f32)] * 2,
-        in_specs=[vmem] * 4 + [smem] * 2,
+        in_specs=[pl.BlockSpec(memory_space=pltpu.HBM)] * 4 + [smem] * 2,
         out_specs=[vmem] * 2,
         scratch_shapes=[
+            pltpu.VMEM((3, rows, ny), f32),
+            pltpu.VMEM((3, rows, ny), f32),
+            pltpu.VMEM((rows, ny), jnp.int32),
+            pltpu.VMEM((len(OFFSETS), rows, ny), jnp.int32),
+            dma((4,)),
             pltpu.VMEM((STEPS, 3, 3 * rows, ny), f32),
             pltpu.VMEM((STEPS, 2, rows, ny), f32),
             pltpu.VMEM((STEPS, 2, 3 * rows, ny), f32),
@@ -348,7 +367,7 @@
             dma((1,)), dma((1,)), dma((4,)), dma((4,)),
         ],
         compiler_params=pltpu.CompilerParams(
-            collective_id=0, has_side_effects=True, vmem_limit_bytes=40 * 1024 * 1024
+            collective_id=0, has_side_effects=True, vmem_limit_bytes=63 * 1024 * 1024 + 960 * 1024
         ),
         name="peridynamics",
     )(

time: 29.8 us -> 27.2 us (0.913)
  local copies, waits for them, and re-layouts: 5.25 us -> 2.01 us
  Pallas kernels: 23.5 us -> 24.3 us
    unnamed x14 -> x4, local copies, waits for them, and re-layouts: 5.25 us -> 2.01 us
    pallas_call x1, Pallas kernels: 23.5 us -> 24.3 us  [on_device(): pl.pallas_call(functools.partial(kernel, (nx, nz, ny)), out_shape=[jax.Sh...]
where the time goes in v3:
time: 27.2 us; the launch traced here: 27 us
  Pallas kernels  24.3 us (89%)
  local copies, waits for them, and re-layouts  2.01 us (7%)
  between operations  0.65 us (2%)
    pallas_call x1, Pallas kernels, on_device(): pl.pallas_call(functools.partial(kernel, (nx, nz, ny)), out_shape=[jax.Sh...  24.3 us
    unnamed x4, local copies, waits for them, and re-layouts  2.01 us

profile of v3, /device:TPU:4, one launch (start us, length us, event | category | flops | bytes accessed | tf_op | source)
XLA Modules:
  0.0 27.0 jit_solution(14037012231549116882)
XLA Ops:
  0.6 24.3 %peridynamics.1 = (f32[3,24,128]{2,1,0:T(8,128)}, f32[3,24,128]{2,1,0:T(8,128)}) custom-call(f32[3,24,128]{2,1,0:T(8,128)} %bitcast.19, f32[3,24,128]{2,1,0:T(8,128)} %bitcast.20, s32[24,128]{1,0:T(8,128)} %bitcast.23, s32[61,24,128]{2,1,0:T(8,128)} %bitcast.18, f32[8]{0:T(128)} %stiff.1, f32[8]{0:T(128)} %crit.1), custom_call_target="tpu_custom_call" | custom-call | tf_op jit(solution)/shard_map/peridynamics/pallas_call | solution.py:339
  24.9 0.0 copy-start
  24.9 1.4 %copy.10 = f32[3,4,6,128]{3,1,2,0:T(4,128)} copy(f32[3,4,6,128]{3,1,2,0:T(4,128)} %bitcast.22) | data formatting | bytes 73728
  26.3 0.0 copy-done
  26.3 0.6 %copy.11 = f32[3,4,6,128]{3,1,2,0:T(4,128)} copy(f32[3,4,6,128]{3,1,2,0:T(4,128)S(1)} %bitcast.21) | data formatting | bytes 73728
Async XLA Ops:
  24.9 1.4 %copy-start = (f32[3,24,128]{2,1,0:T(8,128)S(1)}, f32[3,24,128]{2,1,0:T(8,128)}, u32[]{:S(2)}) copy-start(f32[3,24,128]{2,1,0:T(8,128)} %get-tuple-element.5) | copy-start | bytes 110596

commit v4 on v3

--- a/solution.py
+++ b/solution.py
@@ -178,12 +178,6 @@
     pack_edges([mat_ext[f, own, :] for f in range(2)], mat_send)
     pack_edges([ext[0, f, own, :] for f in range(3)], edge_send.at[0])
 
-    neighbours = lax.select(my_x > 0, 1, 0) + lax.select(my_x < size_x - 1, 1, 0) + 1
-    neighbours = neighbours * (lax.select(my_y > 0, 1, 0) + lax.select(my_y < size_y - 1, 1, 0) + 1) - 1
-    pl.semaphore_wait(barrier, neighbours)
-    start(mat_copies)
-    start(step_copies(0))
-
     reads[3].wait()
 
     def mask_row(k, x):
@@ -197,7 +191,6 @@
             mask_ext[k, pl.ds(rows + x * nz, nz), :] = value
             if x >= nx - d[0]:
                 mask_send[pl.ds(mask_row(k, x - (nx - d[0])), nz), :] = value
-    start(mask_copies())
     for k, d in enumerate(OFFSETS):
         c = d[2]
         if c > 0:
@@ -208,7 +201,14 @@
             down = jnp.where(lane // 4 == ny // 4 - 1 - SLOT[k], roll(value, c - 4 * SLOT[k]), down)
     pack_send[0] = up
     pack_send[1] = down
+
+    neighbours = lax.select(my_x > 0, 1, 0) + lax.select(my_x < size_x - 1, 1, 0) + 1
+    neighbours = neighbours * (lax.select(my_y > 0, 1, 0) + lax.select(my_y < size_y - 1, 1, 0) + 1) - 1
+    pl.semaphore_wait(barrier, neighbours)
+    start(mask_copies())
+    start(mat_copies)
     start(pack_copies())
+    start(step_copies(0))
 
     def shift_fields(source, land, target, count, add_step):
         full = 3 * rows

time: 27.2 us -> 27.2 us (level)
  no operation moved by 1% of the time
where the time goes in v4:
time: 27.2 us; the launch traced here: 27 us
  Pallas kernels  24.3 us (89%)
  local copies, waits for them, and re-layouts  2.01 us (7%)
  between operations  0.65 us (2%)
    pallas_call x1, Pallas kernels, on_device(): pl.pallas_call(functools.partial(kernel, (nx, nz, ny)), out_shape=[jax.Sh...  24.3 us
    unnamed x4, local copies, waits for them, and re-layouts  2.01 us

profile of v4, /device:TPU:4, one launch (start us, length us, event | category | flops | bytes accessed | tf_op | source)
XLA Modules:
  0.0 27.0 jit_solution(16400826983041215937)
XLA Ops:
  0.6 24.3 %peridynamics.1 = (f32[3,24,128]{2,1,0:T(8,128)}, f32[3,24,128]{2,1,0:T(8,128)}) custom-call(f32[3,24,128]{2,1,0:T(8,128)} %bitcast.19, f32[3,24,128]{2,1,0:T(8,128)} %bitcast.20, s32[24,128]{1,0:T(8,128)} %bitcast.23, s32[61,24,128]{2,1,0:T(8,128)} %bitcast.18, f32[8]{0:T(128)} %stiff.1, f32[8]{0:T(128)} %crit.1), custom_call_target="tpu_custom_call" | custom-call | tf_op jit(solution)/shard_map/peridynamics/pallas_call | solution.py:339
  25.0 0.0 copy-start
  25.0 1.4 %copy.10 = f32[3,4,6,128]{3,1,2,0:T(4,128)} copy(f32[3,4,6,128]{3,1,2,0:T(4,128)} %bitcast.22) | data formatting | bytes 73728
  26.4 0.0 copy-done
  26.4 0.6 %copy.11 = f32[3,4,6,128]{3,1,2,0:T(4,128)} copy(f32[3,4,6,128]{3,1,2,0:T(4,128)S(1)} %bitcast.21) | data formatting | bytes 73728
Async XLA Ops:
  25.0 1.4 %copy-start = (f32[3,24,128]{2,1,0:T(8,128)S(1)}, f32[3,24,128]{2,1,0:T(8,128)}, u32[]{:S(2)}) copy-start(f32[3,24,128]{2,1,0:T(8,128)} %get-tuple-element.5) | copy-start | bytes 110596

commit v5 on v3

--- a/solution.py
+++ b/solution.py
@@ -13,6 +13,7 @@
 time_step = 0.05
 MESH = pl.DeviceIdType.MESH
 DIRECTIONS = [(dx, dy) for dx in (-1, 0, 1) for dy in (-1, 0, 1) if (dx, dy) != (0, 0)]
+DIRECTIONS.sort(key=lambda d: -abs(d[0]) - abs(d[1]))
 
 
 def bond_offsets():

time: 27.2 us -> 27.2 us (level)
  no operation moved by 1% of the time
where the time goes in v5:
time: 27.2 us; the launch traced here: 26.9 us
  Pallas kernels  24.2 us (89%)
  local copies, waits for them, and re-layouts  2.01 us (7%)
  between operations  0.65 us (2%)
    pallas_call x1, Pallas kernels, on_device(): pl.pallas_call(functools.partial(kernel, (nx, nz, ny)), out_shape=[jax.Sh...  24.2 us
    unnamed x4, local copies, waits for them, and re-layouts  2.01 us

profile of v5, /device:TPU:4, one launch (start us, length us, event | category | flops | bytes accessed | tf_op | source)
XLA Modules:
  0.0 26.9 jit_solution(17515688488208334354)
XLA Ops:
  0.6 24.2 %peridynamics.1 = (f32[3,24,128]{2,1,0:T(8,128)}, f32[3,24,128]{2,1,0:T(8,128)}) custom-call(f32[3,24,128]{2,1,0:T(8,128)} %bitcast.19, f32[3,24,128]{2,1,0:T(8,128)} %bitcast.20, s32[24,128]{1,0:T(8,128)} %bitcast.23, s32[61,24,128]{2,1,0:T(8,128)} %bitcast.18, f32[8]{0:T(128)} %stiff.1, f32[8]{0:T(128)} %crit.1), custom_call_target="tpu_custom_call" | custom-call | tf_op jit(solution)/shard_map/peridynamics/pallas_call | solution.py:340
  24.8 0.0 copy-start
  24.8 1.4 %copy.10 = f32[3,4,6,128]{3,1,2,0:T(4,128)} copy(f32[3,4,6,128]{3,1,2,0:T(4,128)} %bitcast.22) | data formatting | bytes 73728
  26.2 0.0 copy-done
  26.2 0.6 %copy.11 = f32[3,4,6,128]{3,1,2,0:T(4,128)} copy(f32[3,4,6,128]{3,1,2,0:T(4,128)S(1)} %bitcast.21) | data formatting | bytes 73728
Async XLA Ops:
  24.8 1.4 %copy-start = (f32[3,24,128]{2,1,0:T(8,128)S(1)}, f32[3,24,128]{2,1,0:T(8,128)}, u32[]{:S(2)}) copy-start(f32[3,24,128]{2,1,0:T(8,128)} %get-tuple-element.5) | copy-start | bytes 110596
